TPU v7x, 32 devices: a whole 2x2x4 slice. The times are simulated.
32 devices in a mesh: groups: 2 (over y), space: 16 (over z, x, core).
Axes of the slice: x: 2, y: 2, z: 4, core: 2. Of those that a mesh axis runs over, the one named last changes fastest.
Arguments:
- features: bfloat16 [16384, 256], P(('groups', 'space')), parts along dimension 0, may hold values from -6 to 6
- positions: float32 [3, 16384], P(None, ('groups', 'space')), parts along dimension 1, may hold values from 0 to 1
- k_index: int32 [3, 2048], replicated, may hold values from -8 to 8
- k_filter: bfloat16 [2048, 256], replicated, may hold values from 0.0049743652 to 0.049804688
- w_in: bfloat16 [256, 256], replicated, may hold values from -0.375 to 0.375
- w_out: bfloat16 [256, 256], replicated, may hold values from -0.375 to 0.375
- w_msg: bfloat16 [256, 256], replicated, may hold values from -0.375 to 0.375
- w_short: bfloat16 [256, 256], replicated, may hold values from -0.375 to 0.375
- gamma: float32 [256], replicated, may hold values from 0.02 to 0.5
- ghost_index: int32 [64, 128], P(('groups', 'space')), parts along dimension 0, may hold values from 0 to 511, as said below
- atom_count: int32 [32], P(('groups', 'space')), parts along dimension 0, may hold values from 256 to 512, as said below
- edge_src: int32 [262144], P(('groups', 'space')), parts along dimension 0, may hold values from 0 to 767
- edge_dist: float32 [262144], P(('groups', 'space')), parts along dimension 0, may hold values from 0.5 to 5
- cotangent: bfloat16 [16384, 256], P(('groups', 'space')), parts along dimension 0, may hold values from -6 to 6
Outputs:
- mixed: bfloat16 [16384, 256], P(('groups', 'space')), parts along dimension 0
- feature_grad: bfloat16 [16384, 256], P(('groups', 'space')), parts along dimension 0
There are 2 independent parts, one for each index of `groups`. A program takes and returns all parts, laid end to end along the dimension named above; an argument that names none is the same for every part. Nothing has to cross between parts.
Inputs may be any that keep to these rules, and one draw needn't show every extreme that they name: `ghost_index`: within each row the 128 slots are distinct. `atom_count`: some domain of every cell is full.
All inputs are finite; a program needn't handle non-finite values.
Results may differ from a plain program's by a relative error of at most 0.0065.
Values may be sent and summed in bfloat16 or wider, within the bound.
A program may use at most 128 MiB of HBM per device.

v0:
```python
import functools
import math

import jax
import jax.numpy as jnp
from jax import lax
from jax.experimental import pallas as pl
from jax.experimental.pallas import tpu as pltpu
from jax.sharding import PartitionSpec as P

NEIGH = 16
QUAD = 4
ROWS = 16
F32 = jnp.float32
BF16 = jnp.bfloat16

COS_FIT = (1.0, -19.73920440673828, 64.93911743164062, -85.45014190673828, 60.16762924194336, -25.967599868774414, 6.528658390045166)
SIN_FIT = (6.283185005187988, -41.341590881347656, 81.59994506835938, -76.61447143554688, 41.3428840637207, -12.471243858337402)


def horner(square, coefs):
    result = jnp.full_like(square, coefs[-1])
    for coef in coefs[-2::-1]:
        result = result * square + coef
    return result


def dot(left, right):
    return jnp.dot(left, right, preferred_element_type=F32)


def dot_trail(left, right):
    return lax.dot_general(left, right, (((1,), (1,)), ((), ())), preferred_element_type=F32)


def sigmoid(value):
    return 1.0 / (1.0 + jnp.exp(-value))


def silu_grad(value):
    sig = sigmoid(value)
    return sig * (1.0 + value * (1.0 - sig))


def one_hot(ids, axis, extent):
    shape = (ids.shape[0], extent) if axis == 1 else (extent, ids.shape[1])
    return jnp.where(lax.broadcasted_iota(jnp.int32, shape, axis) == ids, 1.0, 0.0).astype(BF16)


def kernel(
    n,
    scale,
    feat_ref,
    pos_ref,
    kidx_ref,
    kfilt_ref,
    win_ref,
    wout_ref,
    wmsg_ref,
    wshort_ref,
    gamma_ref,
    ghost_ref,
    ghost_col_ref,
    count_ref,
    src_ref,
    src_row_ref,
    dist_ref,
    cot_ref,
    mixed_ref,
    grad_ref,
    phase,
    kcol,
    pos_all,
    quad_all,
    z_send,
    z_recv,
    z_all,
    z_own,
    sib_send,
    sib_recv,
    x_send,
    x_recv,
    table,
    hw,
    agg,
    grad_agg,
    grad_hw,
    ghost_send,
    ghost_back,
    masked_ref,
    glive_ref,
    wave_ref,
    long_ref,
    pos_sems,
    gather_sems,
    zr_sems,
    za_sems,
    quad_sems,
    ghost_sems,
):
    zs = n // QUAD
    at, width = feat_ref.shape
    kq = kidx_ref.shape[1] // QUAD
    kc = kq // zs
    ghost = ghost_ref.shape[1]
    me = lax.axis_index("space")
    q = lax.rem(me, QUAD)
    z = lax.div(me, QUAD)
    base = z * QUAD
    sib = q + 1 - 2 * lax.rem(q, 2)
    xp = lax.rem(q + 2, QUAD)
    diag = lax.rem(sib + 2, QUAD)
    right = lax.rem(me + 1, n)
    left = lax.rem(me + n - 1, n)

    def z_peer(step):
        return lax.rem(z + step, zs)

    barrier = pltpu.get_barrier_semaphore()
    peers = [base + sib, base + xp, left, right] + [z_peer(r) * QUAD + q for r in range(1, zs)]
    for peer in peers:
        pl.semaphore_signal(
            barrier, inc=1, device_id={"space": peer}, device_id_type=pl.DeviceIdType.MESH
        )

    def push(src, dst, sems, index, peer):
        return pltpu.make_async_remote_copy(
            src_ref=src,
            dst_ref=dst,
            send_sem=sems.at[(0,) + index],
            recv_sem=sems.at[(1,) + index],
            device_id={"space": peer},
            device_id_type=pl.DeviceIdType.MESH,
        )

    live = lax.broadcasted_iota(jnp.int32, (at, width), 0) < count_ref[0]
    live_f = jnp.where(live, 1.0, 0.0)
    masked = (feat_ref[...].astype(F32) * live_f).astype(BF16)
    masked_ref[...] = masked
    glive_ref[...] = (cot_ref[...].astype(F32) * live_f).astype(BF16)
    table[pl.ds(0, at), :] = masked
    quad_all[0, q] = dot(masked, win_ref[...]).astype(BF16)
    pos_all[q] = jnp.concatenate([pos_ref[...], jnp.zeros((5, at), F32)], axis=0)
    ghost_send[0, 0] = dot(one_hot(ghost_col_ref[:, 0:1], 1, at), masked).astype(BF16)
    ghost_send[0, 1] = dot(one_hot(ghost_col_ref[:, 1:2], 1, at), masked).astype(BF16)

    pl.semaphore_wait(barrier, len(peers))

    pos_copies = [
        push(pos_all.at[q], pos_all.at[q], pos_sems, (0,), base + sib),
        push(pos_all.at[q], pos_all.at[q], pos_sems, (1,), base + xp),
        push(pos_all.at[xp], pos_all.at[xp], pos_sems, (2,), base + sib),
    ]

    def gather_copies(rnd):
        buf = quad_all.at[rnd]
        return [
            push(buf.at[q], buf.at[q], gather_sems, (rnd, 0), base + sib),
            push(buf.at[q], buf.at[q], gather_sems, (rnd, 1), base + xp),
            push(buf.at[xp], buf.at[xp], gather_sems, (rnd, 2), base + sib),
        ]

    proj_copies = gather_copies(0)
    ghosts_out = [
        push(ghost_send.at[0, 0], table.at[pl.ds(at + ghost, ghost)], ghost_sems, (0, 0), left),
        push(ghost_send.at[0, 1], table.at[pl.ds(at, ghost)], ghost_sems, (0, 1), right),
    ]
    pos_copies[0].start()
    pos_copies[1].start()
    proj_copies[1].start()
    proj_copies[0].start()
    ghosts_out[0].start()
    ghosts_out[1].start()

    kq_rows = kidx_ref[:, pl.ds(pl.multiple_of(q * kq, 128), kq)].astype(F32)
    kcol[...] = jnp.concatenate([kq_rows, jnp.zeros((5, kq), F32)], axis=0).T

    def fill_phase(slot):
        columns = pl.ds(pl.multiple_of(slot * at, 128), at)
        p0 = pos_all[slot, 0:1, :]
        p1 = pos_all[slot, 1:2, :]
        p2 = pos_all[slot, 2:3, :]

        def body(i, carry):
            first = pl.multiple_of(i * ROWS, ROWS)
            ks = kcol[pl.ds(first, ROWS), :]
            turn = ks[:, 0:1] * p0 + ks[:, 1:2] * p1 + ks[:, 2:3] * p2
            turn = turn - jnp.round(turn)
            square = turn * turn
            row = pl.multiple_of(first + lax.div(first, kc) * kc, ROWS)
            phase[pl.ds(row, ROWS), columns] = horner(square, COS_FIT).astype(BF16)
            row = pl.multiple_of(row + kc, ROWS)
            phase[pl.ds(row, ROWS), columns] = (turn * horner(square, SIN_FIT)).astype(BF16)
            return carry

        lax.fori_loop(0, kq // ROWS, body, 0)

    fill_phase(q)
    pos_copies[0].wait()
    pos_copies[1].wait()
    pos_copies[2].start()
    fill_phase(sib)
    fill_phase(xp)
    pos_copies[2].wait()
    proj_copies[1].wait()
    proj_copies[2].start()
    fill_phase(diag)

    def z_start(rnd):
        rows = quad_all[rnd].reshape(QUAD * at, width)
        copies = []
        for r in list(range(1, zs)) + [0]:
            j = z_peer(r)
            part = dot(phase[pl.ds(pl.multiple_of(j * 2 * kc, ROWS), 2 * kc), :], rows)
            if r == 0:
                z_own[...] = part
            else:
                z_send[rnd, j] = part.astype(BF16)
                copy = push(z_send.at[rnd, j], z_recv.at[rnd, z], zr_sems, (rnd, r - 1), j * QUAD + q)
                copy.start()
                copies.append(copy)
        return copies

    def z_middle(rnd, copies):
        total = z_own[...]
        for r in range(1, zs):
            copies[r - 1].wait()
            total = total + z_recv[rnd, lax.rem(z + zs - r, zs)].astype(F32)
        filt = kfilt_ref[pl.ds(pl.multiple_of(q * kq + z * kc, ROWS), kc), :].astype(F32)
        z_all[rnd, z] = (jnp.concatenate([filt, filt], axis=0) * total * scale).astype(BF16)
        out = []
        for r in range(1, zs):
            copy = push(z_all.at[rnd, z], z_all.at[rnd, z], za_sems, (rnd, r - 1), z_peer(r) * QUAD + q)
            copy.start()
            out.append(copy)
        return out

    def z_end(rnd, copies):
        for copy in copies:
            copy.wait()
        spectrum = z_all[rnd].reshape(2 * kq, width).T

        def section(slot):
            return dot(spectrum, phase[:, pl.ds(pl.multiple_of(slot * at, 128), at)])

        across = push(sib_send.at[rnd, 1], sib_recv.at[rnd, 1], quad_sems, (rnd, 0), base + sib)
        beside = push(sib_send.at[rnd, 0], sib_recv.at[rnd, 0], quad_sems, (rnd, 1), base + sib)
        over = push(x_send.at[rnd], x_recv.at[rnd], quad_sems, (rnd, 2), base + xp)
        sib_send[rnd, 1] = section(diag).astype(BF16)
        across.start()
        part = section(xp)
        across.wait()
        x_send[rnd] = (part + sib_recv[rnd, 1].astype(F32)).astype(BF16)
        over.start()
        sib_send[rnd, 0] = section(sib).astype(BF16)
        beside.start()
        part = section(q)
        beside.wait()
        part = part + sib_recv[rnd, 0].astype(F32)
        over.wait()
        return (part + x_recv[rnd].astype(F32)).T

    proj_copies[0].wait()
    proj_copies[2].wait()
    reduce_copies = z_start(0)

    dist = dist_ref[...]
    dist_sq = dist * dist
    turn = dist * 0.1
    live_col = jnp.where(
        lax.broadcasted_iota(jnp.int32, (at, NEIGH), 0) < count_ref[0], 1.0, 0.0
    )
    smooth = live_col * (0.5 * (horner(turn * turn, COS_FIT) + 1.0))
    gamma_neg = -gamma_ref[...]

    def radial(j):
        return smooth[:, j : j + 1] * jnp.exp(gamma_neg * dist_sq[:, j : j + 1])

    ghosts_out[0].wait()
    ghosts_out[1].wait()
    hw[...] = dot(table[...], wmsg_ref[...]).astype(BF16)
    for j in range(NEIGH):
        message = dot(one_hot(src_ref[:, j : j + 1], 1, at + 2 * ghost), hw[...]) * radial(j)
        agg[...] = message if j == 0 else agg[...] + message

    spread_copies = z_middle(0, reduce_copies)

    agg_now = agg[...]
    grad_agg[...] = dot_trail(glive_ref[...], wshort_ref[...]) * silu_grad(agg_now)
    for j in range(NEIGH):
        term = (grad_agg[...] * radial(j)).astype(BF16)
        part = dot(one_hot(src_row_ref[j : j + 1, :], 0, at + 2 * ghost), term)
        grad_hw[...] = part if j == 0 else grad_hw[...] + part

    wave = z_end(0, spread_copies)
    grad_wave = dot_trail(glive_ref[...], wout_ref[...]) * silu_grad(wave)
    quad_all[1, q] = grad_wave.astype(BF16)
    back_copies = gather_copies(1)
    back_copies[1].start()
    back_copies[0].start()

    grad_table = dot_trail(grad_hw[...].astype(BF16), wmsg_ref[...])
    ghost_send[1, 0] = grad_table[at : at + ghost].astype(BF16)
    ghost_send[1, 1] = grad_table[at + ghost :].astype(BF16)
    ghosts_back = [
        push(ghost_send.at[1, 0], ghost_back.at[1], ghost_sems, (1, 0), left),
        push(ghost_send.at[1, 1], ghost_back.at[0], ghost_sems, (1, 1), right),
    ]
    back_copies[1].wait()
    back_copies[2].start()
    ghosts_back[0].start()
    ghosts_back[1].start()
    long_ref[...] = grad_table[:at]
    act = (wave * sigmoid(wave)).astype(BF16)
    short_act = (agg_now * sigmoid(agg_now)).astype(BF16)
    mixed = masked_ref[...].astype(F32) + dot(short_act, wshort_ref[...])
    mixed = mixed + dot(act, wout_ref[...])
    mixed_ref[...] = (live_f * mixed).astype(BF16)
    back_copies[0].wait()
    back_copies[2].wait()
    reduce_copies = z_start(1)

    ghosts_back[0].wait()
    ghosts_back[1].wait()
    own = long_ref[...]
    own = own + dot(one_hot(ghost_ref[0:1, :], 0, at), ghost_back[0])
    own = own + dot(one_hot(ghost_ref[1:2, :], 0, at), ghost_back[1])
    long_ref[...] = own + glive_ref[...].astype(F32)

    spread_copies = z_middle(1, reduce_copies)
    grad_proj = z_end(1, spread_copies).astype(BF16)
    total = long_ref[...] + dot_trail(grad_proj, win_ref[...])
    grad_ref[...] = (live_f * total).astype(BF16)


def shards(n, features, positions, k_index, k_filter, w_in, w_out, w_msg, w_short, gamma,
           ghost_index, atom_count, edge_src, edge_dist, cotangent):
    at, width = features.shape
    ghost = ghost_index.shape[1]
    kv = k_index.shape[1]
    zs = n // QUAD
    kq = kv // QUAD
    kc = kq // zs
    tab = at + 2 * ghost
    src = edge_src.reshape(at, NEIGH)
    vmem = pl.BlockSpec(memory_space=pltpu.VMEM)
    smem = pl.BlockSpec(memory_space=pltpu.SMEM)
    dma = pltpu.SemaphoreType.DMA
    return pl.pallas_call(
        functools.partial(kernel, n, 1.0 / math.sqrt(at * n)),
        out_shape=(
            jax.ShapeDtypeStruct((at, width), BF16),
            jax.ShapeDtypeStruct((at, width), BF16),
        ),
        in_specs=[vmem] * 11 + [smem] + [vmem] * 4,
        out_specs=(vmem, vmem),
        scratch_shapes=[
            pltpu.VMEM((2 * kq, QUAD * at), BF16),
            pltpu.VMEM((kq, 8), F32),
            pltpu.VMEM((QUAD, 8, at), F32),
            pltpu.VMEM((2, QUAD, at, width), BF16),
            pltpu.VMEM((2, zs, 2 * kc, width), BF16),
            pltpu.VMEM((2, zs, 2 * kc, width), BF16),
            pltpu.VMEM((2, zs, 2 * kc, width), BF16),
            pltpu.VMEM((2 * kc, width), F32),
            pltpu.VMEM((2, 2, width, at), BF16),
            pltpu.VMEM((2, 2, width, at), BF16),
            pltpu.VMEM((2, width, at), BF16),
            pltpu.VMEM((2, width, at), BF16),
            pltpu.VMEM((tab, width), BF16),
            pltpu.VMEM((tab, width), BF16),
            pltpu.VMEM((at, width), F32),
            pltpu.VMEM((at, width), F32),
            pltpu.VMEM((tab, width), F32),
            pltpu.VMEM((2, 2, ghost, width), BF16),
            pltpu.VMEM((2, ghost, width), BF16),
            pltpu.VMEM((at, width), BF16),
            pltpu.VMEM((at, width), BF16),
            pltpu.VMEM((at, width), F32),
            pltpu.VMEM((at, width), F32),
            dma((2, 3)),
            dma((2, 2, 3)),
            dma((2, 2, zs - 1)),
            dma((2, 2, zs - 1)),
            dma((2, 2, 3)),
            dma((2, 2, 2)),
        ],
        compiler_params=pltpu.CompilerParams(
            collective_id=0, has_side_effects=True, vmem_limit_bytes=52 * 1024 * 1024
        ),
    )(
        features,
        positions,
        k_index,
        k_filter,
        w_in,
        w_out,
        w_msg,
        w_short,
        gamma.reshape(1, width),
        ghost_index,
        ghost_index.T,
        atom_count,
        src,
        src.T,
        edge_dist.reshape(at, NEIGH),
        cotangent,
    )


def solution(mesh):
    both = ("groups", "space")
    in_specs = (P(both, None), P(None, both)) + (P(),) * 7
    in_specs = in_specs + (P(both, None), P(both), P(both), P(both), P(both, None))
    out_specs = (P(both, None), P(both, None))
    return jax.shard_map(
        functools.partial(shards, mesh.shape["space"]),
        mesh=mesh,
        in_specs=in_specs,
        out_specs=out_specs,
        check_vma=False,
    )
```

profile of v0, /device:TPU:0, one launch (start us, length us, event | category | flops | bytes accessed | tf_op | source)
XLA Modules:
  0.0 106.6 jit_solution(15966780379025301789)
XLA Ops:
  1.3 0.0 copy-start.7
  1.3 0.7 copy-done.7
  2.0 0.0 copy-start.9
  2.0 0.1 copy.18
  2.1 0.6 copy-done.9
  2.7 0.0 copy-start.10
  2.7 0.1 reshape.14.src_ref
  2.9 0.0 copy-start
  2.9 0.0 copy-start.6
  2.9 0.0 copy-start.8
  2.9 0.1 copy.19
  3.0 0.5 copy-done.10
  3.5 0.1 reshape.15.dist_ref
  3.6 0.0 copy-done.3
  3.6 0.1 copy-done.4
  3.7 0.1 copy-done
  3.8 0.0 copy-done.6
  3.8 0.0 copy-done.8
  3.8 0.6 copy-done.1
  4.4 0.0 copy-done.2
  4.5 0.0 copy-done.5
  4.5 100.8 %shard_map.149 = (bf16[512,256]{1,0:T(8,128)(2,1)S(1)}, bf16[512,256]{1,0:T(8,128)(2,1)S(1)}) custom-call(bf16[512,256]{1,0:T(8,128)(2,1)S(1)} %copy-done, f32[3,512]{1,0:T(4,128)S(1)} %copy-done.6, s32[3,2048]{1,0:T(4,128)S(1)} %copy-done.5, bf16[2048,256]{1,0:T(8,128)(2,1)} %kfilt_ref.1, bf16[256,256]{1,0:T(8,128)(2,1)S(1)} %copy-done.1, ...), custom_call_target="tpu_custom_call" | custom-call | tf_op jit(solution)/shard_map/pallas_call | solution.py:349
  105.2 0.7 copy.23
  105.9 0.7 copy.24
  (5 shorter events, 0.0 us)
Async XLA Ops:
  1.3 0.7 copy-start.7
  2.0 0.8 copy-start.9
  2.7 0.8 copy-start.10
  2.7 0.9 copy-start.3
  2.7 1.0 copy-start.4
  2.9 1.0 copy-start
  2.9 1.0 copy-start.6
  2.9 1.0 copy-start.8
  3.5 1.0 copy-start.1
  3.5 1.0 copy-start.2
  3.5 1.0 copy-start.5
where the time goes:
time: 107 us
  Pallas kernels  101 us (94%)
  local copies, waits for them, and re-layouts  4.54 us (4%)
  between operations  1.34 us (1%)
    pallas_call x1, Pallas kernels, shards(): pl.pallas_call(functools.partial(kernel, n, 1.0 / math.sqrt(at * n)), out...  101 us
    unnamed x25, local copies, waits for them, and re-layouts  4.21 us

commit v1 on v0

v1 whole, which is shorter than its diff:
```python
import functools
import math

import jax
import jax.numpy as jnp
from jax import lax
from jax.experimental import pallas as pl
from jax.experimental.pallas import tpu as pltpu
from jax.sharding import PartitionSpec as P

NEIGH = 16
QUAD = 4
HALVES = 2
ROWS = 16
WHOLE = 1.5 * 2.0**23
F32 = jnp.float32
BF16 = jnp.bfloat16

COS_FIT = (0.9999992251396179, -19.738981246948242, 64.92865753173828, -85.27162170410156, 58.79049301147461, -21.07110595703125)
SIN_FIT = (6.283185005187988, -41.341590881347656, 81.59994506835938, -76.61447143554688, 41.3428840637207, -12.471243858337402)


def horner(square, coefs):
    result = jnp.full_like(square, coefs[-1])
    for coef in coefs[-2::-1]:
        result = result * square + coef
    return result


def dot(left, right):
    return jnp.dot(left, right, preferred_element_type=F32)


def dot_trail(left, right):
    return lax.dot_general(left, right, (((1,), (1,)), ((), ())), preferred_element_type=F32)


def sigmoid(value):
    return 1.0 / (1.0 + jnp.exp(-value))


def silu_grad(value):
    sig = sigmoid(value)
    return sig * (1.0 + value * (1.0 - sig))


def one_hot(ids, axis, extent):
    shape = (ids.shape[0], extent) if axis == 1 else (extent, ids.shape[1])
    return jnp.where(lax.broadcasted_iota(jnp.int32, shape, axis) == ids, 1.0, 0.0).astype(BF16)


def kernel(
    n,
    scale,
    feat_ref,
    pos_ref,
    kidx_ref,
    kfilt_ref,
    win_ref,
    wout_ref,
    wmsg_ref,
    wshort_ref,
    gamma_ref,
    ghost_ref,
    ghost_col_ref,
    count_ref,
    src_ref,
    src_row_ref,
    dist_ref,
    cot_ref,
    mixed_ref,
    grad_ref,
    phase,
    kcol,
    pos_all,
    quad_all,
    z_send,
    z_recv,
    z_all,
    z_own,
    sib_send,
    sib_recv,
    x_send,
    x_recv,
    table,
    hw,
    agg,
    grad_agg,
    grad_hw,
    ghost_send,
    ghost_back,
    masked_ref,
    glive_ref,
    wave_ref,
    long_ref,
    upstream_ref,
    mine,
    pos_sems,
    gather_sems,
    zr_sems,
    za_sems,
    quad_sems,
    ghost_sems,
):
    zs = n // QUAD
    at, width = feat_ref.shape
    kq = kidx_ref.shape[1] // QUAD
    kc = kq // zs
    ghost = ghost_ref.shape[1]
    half = width // HALVES
    me = lax.axis_index("space")
    q = lax.rem(me, QUAD)
    z = lax.div(me, QUAD)
    base = z * QUAD
    sib = q + 1 - 2 * lax.rem(q, 2)
    xp = lax.rem(q + 2, QUAD)
    diag = lax.rem(sib + 2, QUAD)
    right = lax.rem(me + 1, n)
    left = lax.rem(me + n - 1, n)

    def z_peer(step):
        return lax.rem(z + step, zs)

    barrier = pltpu.get_barrier_semaphore()
    peers = [base + sib, base + xp, left, right] + [z_peer(r) * QUAD + q for r in range(1, zs)]
    for peer in peers:
        pl.semaphore_signal(
            barrier, inc=1, device_id={"space": peer}, device_id_type=pl.DeviceIdType.MESH
        )

    def push(src, dst, sems, index, peer):
        return pltpu.make_async_remote_copy(
            src_ref=src,
            dst_ref=dst,
            send_sem=sems.at[(0,) + index],
            recv_sem=sems.at[(1,) + index],
            device_id={"space": peer},
            device_id_type=pl.DeviceIdType.MESH,
        )

    live = lax.broadcasted_iota(jnp.int32, (at, width), 0) < count_ref[0]
    live_f = jnp.where(live, 1.0, 0.0)
    masked = (feat_ref[...].astype(F32) * live_f).astype(BF16)
    masked_ref[...] = masked
    pos_all[q] = jnp.concatenate([pos_ref[...], jnp.zeros((5, at), F32)], axis=0)
    proj = dot(masked, win_ref[...]).astype(BF16)
    for h in range(HALVES):
        quad_all[0, h, q] = proj[:, h * half : (h + 1) * half]

    pl.semaphore_wait(barrier, len(peers))

    pos_copies = [
        push(pos_all.at[q], pos_all.at[q], pos_sems, (0,), base + sib),
        push(pos_all.at[q], pos_all.at[q], pos_sems, (1,), base + xp),
        push(pos_all.at[xp], pos_all.at[xp], pos_sems, (2,), base + sib),
    ]

    def gather_copies(rnd, h):
        buf = quad_all.at[rnd, h]
        return [
            push(buf.at[q], buf.at[q], gather_sems, (rnd, h, 0), base + sib),
            push(buf.at[q], buf.at[q], gather_sems, (rnd, h, 1), base + xp),
            push(buf.at[xp], buf.at[xp], gather_sems, (rnd, h, 2), base + sib),
        ]

    pos_copies[1].start()
    pos_copies[0].start()
    gathers = [gather_copies(0, h) for h in range(HALVES)]
    for copies in gathers:
        copies[1].start()
        copies[0].start()

    table[pl.ds(0, at), :] = masked
    ghost_send[0, 0] = dot(one_hot(ghost_col_ref[:, 0:1], 1, at), masked).astype(BF16)
    ghost_send[0, 1] = dot(one_hot(ghost_col_ref[:, 1:2], 1, at), masked).astype(BF16)
    ghosts_out = [
        push(ghost_send.at[0, 0], table.at[pl.ds(at + ghost, ghost)], ghost_sems, (0, 0), left),
        push(ghost_send.at[0, 1], table.at[pl.ds(at, ghost)], ghost_sems, (0, 1), right),
    ]
    ghosts_out[0].start()
    ghosts_out[1].start()
    kq_rows = kidx_ref[:, pl.ds(pl.multiple_of(q * kq, 128), kq)].astype(F32)
    kcol[...] = jnp.concatenate([kq_rows, jnp.zeros((5, kq), F32)], axis=0).T
    glive_ref[...] = (cot_ref[...].astype(F32) * live_f).astype(BF16)
    pos_copies[1].wait()
    pos_copies[2].start()
    pos_copies[0].wait()
    upstream_ref[...] = dot_trail(glive_ref[...], wout_ref[...])
    grad_agg[...] = dot_trail(glive_ref[...], wshort_ref[...])
    pos_copies[2].wait()

    def fill_phase(j):
        def body(i, carry):
            first = pl.multiple_of(j * kc + i * ROWS, ROWS)
            ks = kcol[pl.ds(first, ROWS), :]
            row = pl.multiple_of(j * 2 * kc + i * ROWS, ROWS)
            k0 = jnp.broadcast_to(ks[:, 0:1], (ROWS, at))
            k1 = jnp.broadcast_to(ks[:, 1:2], (ROWS, at))
            k2 = jnp.broadcast_to(ks[:, 2:3], (ROWS, at))
            for slot in range(QUAD):
                columns = pl.ds(slot * at, at)
                turn = k0 * pos_all[slot, 0:1, :] + k1 * pos_all[slot, 1:2, :]
                turn = turn + k2 * pos_all[slot, 2:3, :]
                turn = turn - ((turn + WHOLE) - WHOLE)
                square = turn * turn
                phase[pl.ds(row, ROWS), columns] = horner(square, COS_FIT).astype(BF16)
                sines = (turn * horner(square, SIN_FIT)).astype(BF16)
                phase[pl.ds(pl.multiple_of(row + kc, ROWS), ROWS), columns] = sines
            return carry

        lax.fori_loop(0, kc // ROWS, body, 0)

    def z_part(rnd, h, r):
        j = z_peer(r)
        rows = quad_all[rnd, h].reshape(QUAD * at, half)
        part = dot(phase[pl.ds(pl.multiple_of(j * 2 * kc, ROWS), 2 * kc), :], rows)
        if r == 0:
            z_own[h] = part
            return []
        z_send[rnd, h, j] = part.astype(BF16)
        copy = push(
            z_send.at[rnd, h, j], z_recv.at[rnd, h, z], zr_sems, (rnd, h, r - 1), j * QUAD + q
        )
        copy.start()
        return [copy]

    def z_middle(rnd, h, copies):
        total = z_own[h]
        for r in range(1, zs):
            copies[r - 1].wait()
            total = total + z_recv[rnd, h, lax.rem(z + zs - r, zs)].astype(F32)
        first = pl.multiple_of(q * kq + z * kc, ROWS)
        filt = kfilt_ref[pl.ds(first, kc), h * half : (h + 1) * half].astype(F32)
        z_all[rnd, h, z] = (jnp.concatenate([filt, filt], axis=0) * total * scale).astype(BF16)
        out = []
        for r in range(1, zs):
            copy = push(
                z_all.at[rnd, h, z], z_all.at[rnd, h, z], za_sems, (rnd, h, r - 1), z_peer(r) * QUAD + q
            )
            copy.start()
            out.append(copy)
        return out

    def z_end(rnd, h, copies):
        for copy in copies:
            copy.wait()
        spectrum = z_all[rnd, h].reshape(2 * kq, half).T

        def section(slot):
            return dot(spectrum, phase[:, pl.ds(pl.multiple_of(slot * at, 128), at)])

        def sib_copy(k):
            return push(
                sib_send.at[rnd, h, k], sib_recv.at[rnd, h, k], quad_sems, (rnd, h, k), base + sib
            )

        across, beside = sib_copy(1), sib_copy(0)
        over = push(x_send.at[rnd, h], x_recv.at[rnd, h], quad_sems, (rnd, h, 2), base + xp)
        sib_send[rnd, h, 1] = section(diag).astype(BF16)
        across.start()
        part = section(xp)
        sib_send[rnd, h, 0] = section(sib).astype(BF16)
        beside.start()
        across.wait()
        x_send[rnd, h] = (part + sib_recv[rnd, h, 1].astype(F32)).astype(BF16)
        over.start()
        mine[h] = section(q)
        return beside, over

    def quad_sum(rnd, h, copies):
        copies[0].wait()
        copies[1].wait()
        total = mine[h] + sib_recv[rnd, h, 0].astype(F32)
        return (total + x_recv[rnd, h].astype(F32)).T

    def columns_of(h):
        return pl.ds(h * half, half)

    def back_start(h):
        wave = quad_sum(0, h, sums[h])
        wave_ref[:, columns_of(h)] = wave
        grad_wave = upstream_ref[:, columns_of(h)] * silu_grad(wave)
        quad_all[1, h, q] = grad_wave.astype(BF16)
        copies = gather_copies(1, h)
        copies[1].start()
        copies[0].start()
        return copies

    def forward_on(copies):
        copies[1].wait()
        copies[2].start()

    order = list(range(1, zs)) + [0]
    reduces = [[], []]
    for step, r in enumerate(order):
        fill_phase(z_peer(r))
        if step == 0:
            for copies in gathers:
                forward_on(copies)
            for copies in gathers:
                copies[0].wait()
                copies[2].wait()
        for h in range(HALVES):
            reduces[h] += z_part(0, h, r)

    spreads = [z_middle(0, h, reduces[h]) for h in range(HALVES)]

    dist = dist_ref[...]
    dist_sq = dist * dist
    turn = dist * 0.1
    live_col = jnp.where(
        lax.broadcasted_iota(jnp.int32, (at, NEIGH), 0) < count_ref[0], 1.0, 0.0
    )
    smooth = live_col * (0.5 * (horner(turn * turn, COS_FIT) + 1.0))
    gamma_neg = -gamma_ref[...]

    def radial(j):
        return smooth[:, j : j + 1] * jnp.exp(gamma_neg * dist_sq[:, j : j + 1])

    ghosts_out[0].wait()
    ghosts_out[1].wait()
    hw[...] = dot(table[...], wmsg_ref[...]).astype(BF16)
    for j in range(NEIGH):
        message = dot(one_hot(src_ref[:, j : j + 1], 1, at + 2 * ghost), hw[...]) * radial(j)
        agg[...] = message if j == 0 else agg[...] + message

    def short_back(first, last):
        for j in range(first, last):
            term = (grad_agg[...] * radial(j)).astype(BF16)
            part = dot(one_hot(src_row_ref[j : j + 1, :], 0, at + 2 * ghost), term)
            grad_hw[...] = part if j == 0 else grad_hw[...] + part

    sums = [z_end(0, 0, spreads[0])]
    grad_agg[...] = grad_agg[...] * silu_grad(agg[...])
    short_back(0, 4)
    sums.append(z_end(0, 1, spreads[1]))
    gathers = [back_start(0)]
    short_back(4, 6)
    gathers.append(back_start(1))
    reduces = []
    forward_on(gathers[0])
    gathers[0][0].wait()
    gathers[0][2].wait()
    reduces.append(sum([z_part(1, 0, r) for r in order], []))
    forward_on(gathers[1])
    gathers[1][0].wait()
    gathers[1][2].wait()
    reduces.append(sum([z_part(1, 1, r) for r in order], []))

    short_back(6, NEIGH)
    grad_table = dot_trail(grad_hw[...].astype(BF16), wmsg_ref[...])
    ghost_send[1, 0] = grad_table[at : at + ghost].astype(BF16)
    ghost_send[1, 1] = grad_table[at + ghost :].astype(BF16)
    ghosts_back = [
        push(ghost_send.at[1, 0], ghost_back.at[1], ghost_sems, (1, 0), left),
        push(ghost_send.at[1, 1], ghost_back.at[0], ghost_sems, (1, 1), right),
    ]
    ghosts_back[0].start()
    ghosts_back[1].start()
    long_ref[...] = grad_table[:at]
    spreads = [z_middle(1, h, reduces[h]) for h in range(HALVES)]

    wave = wave_ref[...]
    act = (wave * sigmoid(wave)).astype(BF16)
    short_act = (agg[...] * sigmoid(agg[...])).astype(BF16)
    mixed = masked_ref[...].astype(F32) + dot(short_act, wshort_ref[...])
    mixed = mixed + dot(act, wout_ref[...])
    mixed_ref[...] = (live_f * mixed).astype(BF16)
    ghosts_back[0].wait()
    ghosts_back[1].wait()
    own = long_ref[...]
    own = own + dot(one_hot(ghost_ref[0:1, :], 0, at), ghost_back[0])
    own = own + dot(one_hot(ghost_ref[1:2, :], 0, at), ghost_back[1])
    long_ref[...] = own + glive_ref[...].astype(F32)

    sums = [z_end(1, h, spreads[h]) for h in range(HALVES)]
    grad_proj = [quad_sum(1, h, sums[h]).astype(BF16) for h in range(HALVES)]
    total = long_ref[...] + dot_trail(jnp.concatenate(grad_proj, axis=1), win_ref[...])
    grad_ref[...] = (live_f * total).astype(BF16)


def shards(n, features, positions, k_index, k_filter, w_in, w_out, w_msg, w_short, gamma,
           ghost_index, atom_count, edge_src, edge_dist, cotangent):
    at, width = features.shape
    ghost = ghost_index.shape[1]
    kv = k_index.shape[1]
    zs = n // QUAD
    kq = kv // QUAD
    kc = kq // zs
    tab = at + 2 * ghost
    half = width // HALVES
    src = edge_src.reshape(at, NEIGH)
    vmem = pl.BlockSpec(memory_space=pltpu.VMEM)
    smem = pl.BlockSpec(memory_space=pltpu.SMEM)
    dma = pltpu.SemaphoreType.DMA
    return pl.pallas_call(
        functools.partial(kernel, n, 1.0 / math.sqrt(at * n)),
        out_shape=(
            jax.ShapeDtypeStruct((at, width), BF16),
            jax.ShapeDtypeStruct((at, width), BF16),
        ),
        in_specs=[vmem] * 11 + [smem] + [vmem] * 4,
        out_specs=(vmem, vmem),
        scratch_shapes=[
            pltpu.VMEM((2 * kq, QUAD * at), BF16),
            pltpu.VMEM((kq, 8), F32),
            pltpu.VMEM((QUAD, 8, at), F32),
            pltpu.VMEM((2, HALVES, QUAD, at, half), BF16),
            pltpu.VMEM((2, HALVES, zs, 2 * kc, half), BF16),
            pltpu.VMEM((2, HALVES, zs, 2 * kc, half), BF16),
            pltpu.VMEM((2, HALVES, zs, 2 * kc, half), BF16),
            pltpu.VMEM((HALVES, 2 * kc, half), F32),
            pltpu.VMEM((2, HALVES, 2, half, at), BF16),
            pltpu.VMEM((2, HALVES, 2, half, at), BF16),
            pltpu.VMEM((2, HALVES, half, at), BF16),
            pltpu.VMEM((2, HALVES, half, at), BF16),
            pltpu.VMEM((tab, width), BF16),
            pltpu.VMEM((tab, width), BF16),
            pltpu.VMEM((at, width), F32),
            pltpu.VMEM((at, width), F32),
            pltpu.VMEM((tab, width), F32),
            pltpu.VMEM((2, 2, ghost, width), BF16),
            pltpu.VMEM((2, ghost, width), BF16),
            pltpu.VMEM((at, width), BF16),
            pltpu.VMEM((at, width), BF16),
            pltpu.VMEM((at, width), F32),
            pltpu.VMEM((at, width), F32),
            pltpu.VMEM((at, width), F32),
            pltpu.VMEM((HALVES, half, at), F32),
            dma((2, 3)),
            dma((2, 2, HALVES, 3)),
            dma((2, 2, HALVES, zs - 1)),
            dma((2, 2, HALVES, zs - 1)),
            dma((2, 2, HALVES, 3)),
            dma((2, 2, 2)),
        ],
        compiler_params=pltpu.CompilerParams(
            collective_id=0, has_side_effects=True, vmem_limit_bytes=52 * 1024 * 1024
        ),
    )(
        features,
        positions,
        k_index,
        k_filter,
        w_in,
        w_out,
        w_msg,
        w_short,
        gamma.reshape(1, width),
        ghost_index,
        ghost_index.T,
        atom_count,
        src,
        src.T,
        edge_dist.reshape(at, NEIGH),
        cotangent,
    )


def solution(mesh):
    both = ("groups", "space")
    in_specs = (P(both, None), P(None, both)) + (P(),) * 7
    in_specs = in_specs + (P(both, None), P(both), P(both), P(both), P(both, None))
    out_specs = (P(both, None), P(both, None))
    return jax.shard_map(
        functools.partial(shards, mesh.shape["space"]),
        mesh=mesh,
        in_specs=in_specs,
        out_specs=out_specs,
        check_vma=False,
    )
```

time: 107 us -> 92.1 us (0.86)
  Pallas kernels: 101 us -> 86 us
    pallas_call x1, Pallas kernels: 101 us -> 86 us  [shards(): pl.pallas_call(functools.partial(kernel, n, 1.0 / math.sqrt(at * n)), out...]
where the time goes in v1:
time: 92.1 us; the launch traced here: 91.9 us
  Pallas kernels  86 us (93%)
  local copies, waits for them, and re-layouts  4.54 us (5%)
  between operations  1.34 us (1%)
    pallas_call x1, Pallas kernels, shards(): pl.pallas_call(functools.partial(kernel, n, 1.0 / math.sqrt(at * n)), out...  86 us
    unnamed x25, local copies, waits for them, and re-layouts  4.21 us

profile of v1, /device:TPU:0, one launch (start us, length us, event | category | flops | bytes accessed | tf_op | source)
XLA Modules:
  0.0 91.9 jit_solution(6023403317599984282)
XLA Ops:
  1.3 0.0 copy-start.7
  1.3 0.7 copy-done.7
  2.0 0.0 copy-start.9
  2.0 0.1 copy.18
  2.1 0.6 copy-done.9
  2.7 0.0 copy-start.10
  2.7 0.1 reshape.14.src_ref
  2.9 0.0 copy-start
  2.9 0.0 copy-start.6
  2.9 0.0 copy-start.8
  2.9 0.1 copy.19
  3.0 0.5 copy-done.10
  3.5 0.1 reshape.15.dist_ref
  3.6 0.0 copy-done.3
  3.6 0.1 copy-done.4
  3.7 0.1 copy-done
  3.8 0.0 copy-done.6
  3.8 0.0 copy-done.8
  3.8 0.6 copy-done.1
  4.4 0.0 copy-done.2
  4.5 0.0 copy-done.5
  4.5 86.0 %shard_map.149 = (bf16[512,256]{1,0:T(8,128)(2,1)S(1)}, bf16[512,256]{1,0:T(8,128)(2,1)S(1)}) custom-call(bf16[512,256]{1,0:T(8,128)(2,1)S(1)} %copy-done, f32[3,512]{1,0:T(4,128)S(1)} %copy-done.6, s32[3,2048]{1,0:T(4,128)S(1)} %copy-done.5, bf16[2048,256]{1,0:T(8,128)(2,1)} %kfilt_ref.1, bf16[256,256]{1,0:T(8,128)(2,1)S(1)} %copy-done.1, ...), custom_call_target="tpu_custom_call" | custom-call | tf_op jit(solution)/shard_map/pallas_call | solution.py:396
  90.5 0.7 copy.23
  91.2 0.7 copy.24
  (5 shorter events, 0.0 us)
Async XLA Ops:
  1.3 0.7 copy-start.7
  2.0 0.8 copy-start.9
  2.7 0.8 copy-start.10
  2.7 0.9 %copy-start.3 = (bf16[256,256]{1,0:T(8,128)(2,1)S(1)}, bf16[256,256]{1,0:T(8,128)(2,1)}, u32[]{:S(2)}) copy-start(bf16[256,256]{1,0:T(8,128)(2,1)} %wmsg_ref.1) | copy-start | bytes 393220
  2.7 1.0 %copy-start.4 = (bf16[256,256]{1,0:T(8,128)(2,1)S(1)}, bf16[256,256]{1,0:T(8,128)(2,1)}, u32[]{:S(2)}) copy-start(bf16[256,256]{1,0:T(8,128)(2,1)} %wshort_ref.1) | copy-start | bytes 393220
  2.9 1.0 %copy-start = (bf16[512,256]{1,0:T(8,128)(2,1)S(1)}, bf16[512,256]{1,0:T(8,128)(2,1)}, u32[]{:S(2)}) copy-start(bf16[512,256]{1,0:T(8,128)(2,1)} %feat_ref.1) | copy-start | bytes 786436
  2.9 1.0 %copy-start.6 = (f32[3,512]{1,0:T(4,128)S(1)}, f32[3,512]{1,0:T(4,128)}, u32[]{:S(2)}) copy-start(f32[3,512]{1,0:T(4,128)} %pos_ref.1) | copy-start | bytes 18436
  2.9 1.0 %copy-start.8 = (f32[256]{0:T(256)S(1)}, f32[256]{0:T(256)}, u32[]{:S(2)}) copy-start(f32[256]{0:T(256)} %param.22) | copy-start | bytes 3076
  3.5 1.0 %copy-start.1 = (bf16[256,256]{1,0:T(8,128)(2,1)S(1)}, bf16[256,256]{1,0:T(8,128)(2,1)}, u32[]{:S(2)}) copy-start(bf16[256,256]{1,0:T(8,128)(2,1)} %win_ref.1) | copy-start | bytes 393220
  3.5 1.0 %copy-start.2 = (bf16[256,256]{1,0:T(8,128)(2,1)S(1)}, bf16[256,256]{1,0:T(8,128)(2,1)}, u32[]{:S(2)}) copy-start(bf16[256,256]{1,0:T(8,128)(2,1)} %wout_ref.1) | copy-start | bytes 393220
  3.5 1.0 %copy-start.5 = (s32[3,2048]{1,0:T(4,128)S(1)}, s32[3,2048]{1,0:T(4,128)}, u32[]{:S(2)}) copy-start(s32[3,2048]{1,0:T(4,128)} %kidx_ref.1) | copy-start | bytes 73732

commit v2 on v1

--- a/solution.py
+++ b/solution.py
@@ -62,10 +62,8 @@
     wshort_ref,
     gamma_ref,
     ghost_ref,
-    ghost_col_ref,
     count_ref,
     src_ref,
-    src_row_ref,
     dist_ref,
     cot_ref,
     mixed_ref,
@@ -78,6 +76,7 @@
     z_recv,
     z_all,
     z_own,
+    z_keep,
     sib_send,
     sib_recv,
     x_send,
@@ -171,8 +170,10 @@
         copies[0].start()
 
     table[pl.ds(0, at), :] = masked
-    ghost_send[0, 0] = dot(one_hot(ghost_col_ref[:, 0:1], 1, at), masked).astype(BF16)
-    ghost_send[0, 1] = dot(one_hot(ghost_col_ref[:, 1:2], 1, at), masked).astype(BF16)
+    ghost_pad = jnp.concatenate([ghost_ref[...].astype(F32), jnp.zeros((6, ghost), F32)], axis=0)
+    ghost_col = ghost_pad.T.astype(jnp.int32)
+    ghost_send[0, 0] = dot(one_hot(ghost_col[:, 0:1], 1, at), masked).astype(BF16)
+    ghost_send[0, 1] = dot(one_hot(ghost_col[:, 1:2], 1, at), masked).astype(BF16)
     ghosts_out = [
         push(ghost_send.at[0, 0], table.at[pl.ds(at + ghost, ghost)], ghost_sems, (0, 0), left),
         push(ghost_send.at[0, 1], table.at[pl.ds(at, ghost)], ghost_sems, (0, 1), right),
@@ -210,40 +211,74 @@
 
         lax.fori_loop(0, kc // ROWS, body, 0)
 
-    def z_part(rnd, h, r):
-        j = z_peer(r)
+    paired = zs == 4
+    if paired:
+        z1 = z + 1 - 2 * lax.rem(z, 2)
+        z2 = lax.rem(z + 2, zs)
+        targets = [lax.rem(z1 + 2, zs), z2, z1, z]
+    else:
+        targets = [z_peer(r) for r in range(1, zs)] + [z]
+
+    def z_part(rnd, h, step):
+        j = targets[step]
         rows = quad_all[rnd, h].reshape(QUAD * at, half)
         part = dot(phase[pl.ds(pl.multiple_of(j * 2 * kc, ROWS), 2 * kc), :], rows)
-        if r == 0:
+        if step == zs - 1:
             z_own[h] = part
             return []
+        if paired and step == 1:
+            z_keep[h] = part
+            return []
         z_send[rnd, h, j] = part.astype(BF16)
+        to, slot, index = (z1, step // 2, step // 2) if paired else (j, z, step)
         copy = push(
-            z_send.at[rnd, h, j], z_recv.at[rnd, h, z], zr_sems, (rnd, h, r - 1), j * QUAD + q
+            z_send.at[rnd, h, j], z_recv.at[rnd, h, slot], zr_sems, (rnd, h, index), to * QUAD + q
         )
         copy.start()
         return [copy]
 
+    def z_fold(rnd, h, copies):
+        if not paired:
+            return
+        copies[0].wait()
+        z_send[rnd, h, z2] = (z_keep[h] + z_recv[rnd, h, 0].astype(F32)).astype(BF16)
+        copy = push(
+            z_send.at[rnd, h, z2], z_recv.at[rnd, h, 2], zr_sems, (rnd, h, 2), z2 * QUAD + q
+        )
+        copy.start()
+        copies.append(copy)
+
     def z_middle(rnd, h, copies):
         total = z_own[h]
         for r in range(1, zs):
+            if paired and r == 1:
+                continue
             copies[r - 1].wait()
-            total = total + z_recv[rnd, h, lax.rem(z + zs - r, zs)].astype(F32)
+            slot = r - 1 if paired else lax.rem(z + zs - r, zs)
+            total = total + z_recv[rnd, h, slot].astype(F32)
         first = pl.multiple_of(q * kq + z * kc, ROWS)
         filt = kfilt_ref[pl.ds(first, kc), h * half : (h + 1) * half].astype(F32)
         z_all[rnd, h, z] = (jnp.concatenate([filt, filt], axis=0) * total * scale).astype(BF16)
+        own = z_all.at[rnd, h, z]
+        peers_of = [z1, z2] if paired else targets[:-1]
         out = []
-        for r in range(1, zs):
-            copy = push(
-                z_all.at[rnd, h, z], z_all.at[rnd, h, z], za_sems, (rnd, h, r - 1), z_peer(r) * QUAD + q
-            )
-            copy.start()
-            out.append(copy)
+        for index, peer in enumerate(peers_of):
+            out.append(push(own, own, za_sems, (rnd, h, index), peer * QUAD + q))
+            out[index].start()
         return out
 
+    def z_relay(rnd, h, copies):
+        if not paired:
+            return
+        copies[1].wait()
+        slot = z_all.at[rnd, h, z2]
+        copies.append(push(slot, slot, za_sems, (rnd, h, 2), z1 * QUAD + q))
+        copies[2].start()
+
     def z_end(rnd, h, copies):
-        for copy in copies:
-            copy.wait()
+        for index, copy in enumerate(copies):
+            if not (paired and index == 1):
+                copy.wait()
         spectrum = z_all[rnd, h].reshape(2 * kq, half).T
 
         def section(slot):
@@ -290,10 +325,9 @@
         copies[1].wait()
         copies[2].start()
 
-    order = list(range(1, zs)) + [0]
     reduces = [[], []]
-    for step, r in enumerate(order):
-        fill_phase(z_peer(r))
+    for step in range(zs):
+        fill_phase(targets[step])
         if step == 0:
             for copies in gathers:
                 forward_on(copies)
@@ -301,7 +335,10 @@
                 copies[0].wait()
                 copies[2].wait()
         for h in range(HALVES):
-            reduces[h] += z_part(0, h, r)
+            reduces[h] += z_part(0, h, step)
+        if step == zs - 2:
+            for h in range(HALVES):
+                z_fold(0, h, reduces[h])
 
     spreads = [z_middle(0, h, reduces[h]) for h in range(HALVES)]
 
@@ -323,11 +360,17 @@
     for j in range(NEIGH):
         message = dot(one_hot(src_ref[:, j : j + 1], 1, at + 2 * ghost), hw[...]) * radial(j)
         agg[...] = message if j == 0 else agg[...] + message
+        if j == 7:
+            z_relay(0, 0, spreads[0])
+    z_relay(0, 1, spreads[1])
+
+    src_pad = jnp.concatenate([src_ref[...].astype(F32), jnp.zeros((at, 128 - NEIGH), F32)], axis=1)
+    src_row = src_pad.T[:NEIGH].astype(jnp.int32)
 
     def short_back(first, last):
         for j in range(first, last):
             term = (grad_agg[...] * radial(j)).astype(BF16)
-            part = dot(one_hot(src_row_ref[j : j + 1, :], 0, at + 2 * ghost), term)
+            part = dot(one_hot(src_row[j : j + 1, :], 0, at + 2 * ghost), term)
             grad_hw[...] = part if j == 0 else grad_hw[...] + part
 
     sums = [z_end(0, 0, spreads[0])]
@@ -341,11 +384,13 @@
     forward_on(gathers[0])
     gathers[0][0].wait()
     gathers[0][2].wait()
-    reduces.append(sum([z_part(1, 0, r) for r in order], []))
+    reduces.append(sum([z_part(1, 0, step) for step in range(zs)], []))
     forward_on(gathers[1])
     gathers[1][0].wait()
     gathers[1][2].wait()
-    reduces.append(sum([z_part(1, 1, r) for r in order], []))
+    reduces.append(sum([z_part(1, 1, step) for step in range(zs)], []))
+    for h in range(HALVES):
+        z_fold(1, h, reduces[h])
 
     short_back(6, NEIGH)
     grad_table = dot_trail(grad_hw[...].astype(BF16), wmsg_ref[...])
@@ -363,6 +408,7 @@
     wave = wave_ref[...]
     act = (wave * sigmoid(wave)).astype(BF16)
     short_act = (agg[...] * sigmoid(agg[...])).astype(BF16)
+    z_relay(1, 0, spreads[0])
     mixed = masked_ref[...].astype(F32) + dot(short_act, wshort_ref[...])
     mixed = mixed + dot(act, wout_ref[...])
     mixed_ref[...] = (live_f * mixed).astype(BF16)
@@ -373,6 +419,7 @@
     own = own + dot(one_hot(ghost_ref[1:2, :], 0, at), ghost_back[1])
     long_ref[...] = own + glive_ref[...].astype(F32)
 
+    z_relay(1, 1, spreads[1])
     sums = [z_end(1, h, spreads[h]) for h in range(HALVES)]
     grad_proj = [quad_sum(1, h, sums[h]).astype(BF16) for h in range(HALVES)]
     total = long_ref[...] + dot_trail(jnp.concatenate(grad_proj, axis=1), win_ref[...])
@@ -399,7 +446,7 @@
             jax.ShapeDtypeStruct((at, width), BF16),
             jax.ShapeDtypeStruct((at, width), BF16),
         ),
-        in_specs=[vmem] * 11 + [smem] + [vmem] * 4,
+        in_specs=[vmem] * 10 + [smem] + [vmem] * 3,
         out_specs=(vmem, vmem),
         scratch_shapes=[
             pltpu.VMEM((2 * kq, QUAD * at), BF16),
@@ -409,6 +456,7 @@
             pltpu.VMEM((2, HALVES, zs, 2 * kc, half), BF16),
             pltpu.VMEM((2, HALVES, zs, 2 * kc, half), BF16),
             pltpu.VMEM((2, HALVES, zs, 2 * kc, half), BF16),
+            pltpu.VMEM((HALVES, 2 * kc, half), F32),
             pltpu.VMEM((HALVES, 2 * kc, half), F32),
             pltpu.VMEM((2, HALVES, 2, half, at), BF16),
             pltpu.VMEM((2, HALVES, 2, half, at), BF16),
@@ -448,10 +496,8 @@
         w_short,
         gamma.reshape(1, width),
         ghost_index,
-        ghost_index.T,
         atom_count,
         src,
-        src.T,
         edge_dist.reshape(at, NEIGH),
         cotangent,
     )

time: 92.1 us -> 92.2 us (level)
    unnamed x25 -> x20, local copies, waits for them, and re-layouts: 4.21 us -> 3.25 us
where the time goes in v2:
time: 92.2 us; the launch traced here: 92 us
  Pallas kernels  85.4 us (93%)
  local copies, waits for them, and re-layouts  5.09 us (6%)
  between operations  1.42 us (2%)
    pallas_call x1, Pallas kernels, shards(): pl.pallas_call(functools.partial(kernel, n, 1.0 / math.sqrt(at * n)), out...  85.4 us
    unnamed x20, local copies, waits for them, and re-layouts  3.25 us

profile of v2, /device:TPU:0, one launch (start us, length us, event | category | flops | bytes accessed | tf_op | source)
XLA Modules:
  0.0 92.0 jit_solution(15212248070614875166)
XLA Ops:
  1.3 0.0 copy-start
  1.3 0.0 copy-start.6
  1.3 0.0 copy-start.7
  1.3 0.0 copy-start.8
  1.3 0.9 reshape.14.src_ref
  2.2 0.0 copy-start.1
  2.3 0.0 copy-start.2
  2.3 0.0 copy-start.5
  2.3 0.9 %reshape.15.dist_ref = f32[512,16]{1,0:T(8,128)S(1)} reshape(f32[8192]{0:T(1024)} %param.26) | data formatting | bytes 65536 | tf_op jit(solution)/shard_map/reshape | solution.py:501
  3.2 0.0 copy-done
  3.2 0.0 copy-done.6
  3.2 0.0 copy-done.7
  3.2 0.0 copy-done.8
  3.3 0.0 copy-done.1
  3.3 0.0 copy-done.2
  3.3 0.0 copy-done.5
  3.3 0.0 copy-start.3
  3.3 0.9 copy-done.3
  4.2 0.0 copy-start.4
  4.2 0.9 copy-done.4
  5.1 85.4 %shard_map.149 = (bf16[512,256]{1,0:T(8,128)(2,1)S(1)}, bf16[512,256]{1,0:T(8,128)(2,1)S(1)}) custom-call(bf16[512,256]{1,0:T(8,128)(2,1)S(1)} %copy-done, f32[3,512]{1,0:T(4,128)S(1)} %copy-done.6, s32[3,2048]{1,0:T(4,128)S(1)} %copy-done.5, bf16[2048,256]{1,0:T(8,128)(2,1)} %kfilt_ref.1, bf16[256,256]{1,0:T(8,128)(2,1)S(1)} %copy-done.1, ...), custom_call_target="tpu_custom_call" | custom-call | tf_op jit(solution)/shard_map/pallas_call | solution.py:443
  90.5 0.7 copy.19
  91.3 0.7 copy.20
Async XLA Ops:
  1.3 1.9 %copy-start = (bf16[512,256]{1,0:T(8,128)(2,1)S(1)}, bf16[512,256]{1,0:T(8,128)(2,1)}, u32[]{:S(2)}) copy-start(bf16[512,256]{1,0:T(8,128)(2,1)} %feat_ref.1) | copy-start | bytes 786436
  1.3 1.9 %copy-start.6 = (f32[3,512]{1,0:T(4,128)S(1)}, f32[3,512]{1,0:T(4,128)}, u32[]{:S(2)}) copy-start(f32[3,512]{1,0:T(4,128)} %pos_ref.1) | copy-start | bytes 18436
  1.3 1.9 %copy-start.7 = (f32[256]{0:T(256)S(1)}, f32[256]{0:T(256)}, u32[]{:S(2)}) copy-start(f32[256]{0:T(256)} %param.22) | copy-start | bytes 3076
  1.3 1.9 %copy-start.8 = (s32[2,128]{1,0:T(2,128)S(1)}, s32[2,128]{1,0:T(2,128)}, u32[]{:S(2)}) copy-start(s32[2,128]{1,0:T(2,128)} %ghost_ref.1) | copy-start | bytes 3076
  2.2 1.0 %copy-start.1 = (bf16[256,256]{1,0:T(8,128)(2,1)S(1)}, bf16[256,256]{1,0:T(8,128)(2,1)}, u32[]{:S(2)}) copy-start(bf16[256,256]{1,0:T(8,128)(2,1)} %win_ref.1) | copy-start | bytes 393220
  2.3 1.0 %copy-start.2 = (bf16[256,256]{1,0:T(8,128)(2,1)S(1)}, bf16[256,256]{1,0:T(8,128)(2,1)}, u32[]{:S(2)}) copy-start(bf16[256,256]{1,0:T(8,128)(2,1)} %wout_ref.1) | copy-start | bytes 393220
  2.3 1.0 %copy-start.5 = (s32[3,2048]{1,0:T(4,128)S(1)}, s32[3,2048]{1,0:T(4,128)}, u32[]{:S(2)}) copy-start(s32[3,2048]{1,0:T(4,128)} %kidx_ref.1) | copy-start | bytes 73732
  3.3 0.9 copy-start.3
  4.2 0.9 copy-start.4
